TPU v7x, 32 devices: a whole 2x2x4 slice. The times are simulated.
32 devices in a mesh: ma: 16 (over z, x, core), bl: 2 (over y).
Axes of the slice: x: 2, y: 2, z: 4, core: 2. Of those that a mesh axis runs over, the one named last changes fastest.
Arguments:
- visibilities: bfloat16 [2, 4160, 8192], P(None, 'bl', 'ma'), may hold values from -6 to 6
- beam_blocks: bfloat16 [16, 2, 4160, 1000], P('ma', None, 'bl'), may hold values from -0.125 to 0.125
- feed_pairs: int32 [4160, 2], P('bl'), may hold values from 0 to 1023
- feed_gains: float32 [2, 1024], replicated, may hold values from -1.5 to 1.5
- m_order: int32 [16], replicated, may hold values from 0 to 15, each once
Outputs:
- sky_modes: float32 [2, 16, 1000], P(None, 'ma', 'bl')
All inputs are finite; a program needn't handle non-finite values.
Results may differ from a plain program's by a relative error of at most 0.0049.
Values may be sent and summed in bfloat16 or wider, within the bound.
A program may use at most 64 MiB of HBM per device.

v0:
```python
import jax
import jax.numpy as jnp
from jax import lax
from jax.sharding import PartitionSpec as P

NT = 8192


def dft_weights(time_index, m_values):
    wrapped = jnp.mod(time_index[:, None] * m_values[None, :], NT).astype(jnp.float32)
    phases = wrapped * (2.0 * jnp.pi / NT)
    scale = 1.0 / jnp.sqrt(jnp.float32(NT))
    cos_part = (jnp.cos(phases) * scale).astype(jnp.bfloat16)
    sin_part = (jnp.sin(phases) * scale).astype(jnp.bfloat16)
    upper = jnp.concatenate([cos_part, -sin_part], axis=1)
    lower = jnp.concatenate([sin_part, cos_part], axis=1)
    return jnp.concatenate([upper, lower], axis=0)


def transform(visible, weights, count):
    stacked_in = jnp.concatenate([visible[0], visible[1]], axis=1)
    flat = jnp.dot(stacked_in, weights, preferred_element_type=jnp.float32)
    return jnp.stack([flat[:, :count], flat[:, count:]])


def per_device(visibilities, beam_blocks, feed_pairs, feed_gains, m_order):
    count = m_order.shape[0]
    m_values = m_order - count // 2
    local_times = visibilities.shape[2]
    first_time = lax.axis_index("ma") * local_times
    time_index = first_time + jnp.arange(local_times, dtype=jnp.int32)
    weights = dft_weights(time_index, m_values)
    partial_spectra = transform(visibilities, weights, count)
    owned = lax.psum_scatter(partial_spectra, "ma", scatter_dimension=2, tiled=True).astype(
        jnp.bfloat16
    )
    local_rows = feed_pairs.shape[0]
    feed_count = feed_gains.shape[1]
    both_feeds = jnp.concatenate([feed_pairs[:, 0], feed_pairs[:, 1]], axis=0)
    feed_iota = jnp.arange(feed_count, dtype=jnp.int32)
    one_hot = (both_feeds[:, None] == feed_iota[None, :]).astype(jnp.float32)
    picked = jnp.dot(
        one_hot,
        jnp.transpose(feed_gains),
        precision=lax.Precision.HIGHEST,
        preferred_element_type=jnp.float32,
    )
    a_re = picked[:local_rows, 0]
    a_im = picked[:local_rows, 1]
    b_re = picked[local_rows:, 0]
    b_im = picked[local_rows:, 1]
    factor_re = (a_re * b_re + a_im * b_im)[:, None]
    factor_im = (a_im * b_re - a_re * b_im)[:, None]
    spec_re = owned[0].astype(jnp.float32)
    spec_im = owned[1].astype(jnp.float32)
    weighted_re = (spec_re * factor_re - spec_im * factor_im).astype(jnp.bfloat16)
    weighted_im = (spec_re * factor_im + spec_im * factor_re).astype(jnp.bfloat16)
    row_real = jnp.concatenate([weighted_re, weighted_im], axis=0)
    row_imag = jnp.concatenate([weighted_im, -weighted_re], axis=0)
    vectors = jnp.transpose(jnp.stack([row_real, row_imag]), (2, 0, 1))
    local_modes = beam_blocks.shape[0]
    block_rows = beam_blocks.shape[2]
    width = beam_blocks.shape[3]
    flat_blocks = beam_blocks.reshape(local_modes, 2 * block_rows, width)
    partial_value = jnp.einsum(
        "mkc,mcl->kml", vectors, flat_blocks, preferred_element_type=jnp.float32
    )
    totals = lax.psum(partial_value, "bl")
    share_width = width // lax.axis_size("bl")
    result = lax.dynamic_slice_in_dim(totals, lax.axis_index("bl") * share_width, share_width, 2)
    return result


def solution(mesh):
    return jax.shard_map(
        per_device,
        mesh=mesh,
        in_specs=(P(None, "bl", "ma"), P("ma", None, "bl", None), P("bl", None), P(), P()),
        out_specs=P(None, "ma", "bl"),
        check_vma=False,
    )
```

profile of v0, /device:TPU:0, one launch (start us, length us, event | category | flops | bytes accessed | tf_op | source)
XLA Modules:
  0.0 91.0 jit_solution(16158775713219875972)
XLA Ops:
  0.0 0.0 copy-start
  0.0 0.7 broadcast_add_fusion
  0.7 0.2 multiply_convert_fusion
  0.9 0.2 fusion.20
  1.1 2.5 %slice_bitcast_fusion.1 = (bf16[2080,512]{1,0:T(8,128)(2,1)S(1)}, bf16[2080,512]{1,0:T(8,128)(2,1)S(1)}) fusion(bf16[2,2080,512]{2,1,0:T(8,128)(2,1)} %param.5), kind=kLoop, calls=%fused_computation.8 | loop fusion | bytes 8519680 | tf_op jit(solution)/shard_map/squeeze | solution.py:21
  3.6 0.0 copy-start.2
  3.6 0.0 copy-start.1
  3.7 1.3 %fusion.2 = f32[2080,32]{0,1:T(8,128)S(1)} fusion(bf16[2080,512]{1,0:T(8,128)(2,1)S(1)} %get-tuple-element.13, bf16[2080,512]{1,0:T(8,128)(2,1)S(1)} %get-tuple-element.12, bf16[512,16]{0,1:T(8,128)(2,1)S(1)} %get-tuple-element.19, bf16[512,16]{0,1:T(8,128)(2,1)S(1)} %get-tuple-element.18, bf16[512,16]{0,1:T(8,128)(2,1)S(1)} %fusion.20), kind=kOutput, calls=%fused_computation.3 | convolution fusion | flops 145096704 | bytes 4575232 | tf_op jit(solution)/shard_map/dot_general | solution.py:22
  5.1 0.1 copy.8
  5.2 66.1 %all-reduce.2 = bf16[2,2080,16]{1,0,2:T(2,128)(2,1)S(1)} all-reduce(f32[2,2080,16]{1,0,2:T(2,128)S(1)} %copy.8), channel_id=2, replica_groups=mesh['ma'=16,'bl'=2] {'ma'}, use_global_device_ids=true, to_apply=%region_0.1.clone | all-reduce | flops 66560 | bytes 399360
  71.4 0.0 copy-done.2
  71.4 0.6 dynamic-slice
  72.0 0.7 dynamic-slice_convert_fusion
  72.6 0.0 copy-done.1
  72.7 0.1 pad_add_fusion
  72.8 0.0 copy-done
  72.8 7.6 %fusion = f32[4160,2]{0,1:T(2,128)S(1)} fusion(f32[2,1024]{1,0:T(2,128)S(1)} %copy-done, s32[4160]{0:T(1024)S(1)} %pad_add_fusion), kind=kOutput, calls=%fused_computation.1 | convolution fusion | flops 106496000 | bytes 58112 | tf_op jit(solution)/shard_map/dot_general | solution.py:42
  80.4 0.1 add_convert_fusion
  80.5 0.1 maximum_bitcast_fusion
  80.6 0.1 pad_maximum_fusion.1
  80.7 4.6 %convolution_bitcast_fusion = f32[2,1,1000]{2,0,1:T(2,128)S(1)} fusion(bf16[4160,1000]{1,0:T(8,128)(2,1)} %bitcast.45, bf16[2,4160,1]{1,2,0:T(2,128)(2,1)S(1)} %pad_maximum_fusion.1), kind=kOutput, calls=%fused_computation.9 | convolution fusion | flops 16640000 | bytes 8344640 | tf_op jit(solution)/shard_map/mkc,mcl->kml/dot_general | solution.py:65
  85.3 5.0 %psum.7 = f32[2,1,1000]{2,0,1:T(2,128)S(1)} all-reduce(f32[2,1,1000]{2,0,1:T(2,128)S(1)} %convolution_bitcast_fusion), channel_id=1, replica_groups=mesh['ma'=16,'bl'=2] {'bl'}, use_global_device_ids=true, to_apply=%region_1.2 | all-reduce | flops 2000 | bytes 16000 | tf_op jit(solution)/shard_map/psum | solution.py:68
  90.3 0.1 constant_dynamic-slice_fusion
  90.4 0.6 copy.9
  (5 shorter events, 0.1 us)
Async XLA Ops:
  0.0 72.8 %copy-start = (f32[2,1024]{1,0:T(2,128)S(1)}, f32[2,1024]{1,0:T(2,128)}, u32[]{:S(2)}) copy-start(f32[2,1024]{1,0:T(2,128)} %param.8) | copy-start | bytes 24580
  3.6 67.8 %copy-start.2 = (u32[32]{0:T(128)S(1)}, u32[32]{0:T(128)}, u32[]{:S(2)}) copy-start(u32[32]{0:T(128)} %constant.40) | copy-start | bytes 388
  3.6 69.0 %copy-start.1 = (s32[2080,2]{0,1:T(2,128)S(1)}, s32[2080,2]{0,1:T(2,128)}, u32[]{:S(2)}) copy-start(s32[2080,2]{0,1:T(2,128)} %param.7) | copy-start | bytes 49924
where the time goes:
time: 91.2 us; the launch traced here: 91 us
  blocking collectives  71.1 us (78%)
  matrix products  13.6 us (15%)
  local copies, waits for them, and re-layouts  4.68 us (5%)
  other arithmetic  1.49 us (2%)
    unnamed x1, blocking collectives  66.1 us
    dot_general x1, matrix products, per_device(): jnp.dot(one_hot, jnp.transpose(feed_gains), precision=lax.Precision.HIGHE...  7.6 us
    psum x1, blocking collectives, per_device(): totals = lax.psum(partial_value, 'bl')  4.97 us
    dot_general x1, matrix products, per_device(): jnp.einsum('mkc,mcl->kml', vectors, flat_blocks, preferred_element_type=j...  4.63 us
    squeeze x1, local copies, waits for them, and re-layouts, transform(): stacked_in = jnp.concatenate([visible[0], visible[1]], axis=1)  2.52 us

commit v1 on v0

v1 whole, which is shorter than its diff:
```python
import functools

import jax
import jax.numpy as jnp
import numpy as np
from jax import lax
from jax.experimental import pallas as pl
from jax.experimental.pallas import tpu as pltpu
from jax.sharding import PartitionSpec as P

NT = 8192
LANES = 128
CHUNKS = 2
MESH = pl.DeviceIdType.MESH


def trig(k):
    quarter = NT // 4
    turn = (k + quarter // 2) // quarter
    x = (k - turn * quarter).astype(jnp.float32) * np.float32(2.0 * np.pi / NT)
    y = x * x
    sin_x = x * (1.0 + y * (-1.0 / 6 + y * (1.0 / 120 + y * (-1.0 / 5040 + y * (1.0 / 362880)))))
    cos_x = 1.0 + y * (-0.5 + y * (1.0 / 24 + y * (-1.0 / 720 + y * (1.0 / 40320))))
    odd = (turn & 1) == 1
    cos_k = jnp.where(odd, sin_x, cos_x)
    sin_k = jnp.where(odd, cos_x, sin_x)
    cos_k = jnp.where(((turn + 1) & 2) == 2, -cos_k, cos_k)
    sin_k = jnp.where((turn & 2) == 2, -sin_k, sin_k)
    return cos_k, sin_k


def peer_order(count):
    return sorted(range(1, count), key=lambda k: abs(k - count // 2))


def kernel(
    n_ma, n_bl, vis, beam, pairs, gains, order, out,
    vis_v, beam_v, pairs_v, gains_v, order_s,
    sums, part, got, rem_part, rem_got, table, factor, lhs, share, share_got,
    vis_sem, beam_sem, small_sem, send_sem, recv_sem, rem_send, rem_recv, bl_send, bl_recv,
):
    me = lax.axis_index("ma")
    my_bl = lax.axis_index("bl")
    rows = vis.shape[1]
    local_times = vis.shape[2]
    cols = rows // LANES
    rem = rows - cols * LANES
    per = cols // CHUNKS
    peers = [lax.rem(me + k, n_ma) for k in range(n_ma)]
    order_of = peer_order(n_ma)

    barrier = pltpu.get_barrier_semaphore()
    for k in range(1, n_ma):
        pl.semaphore_signal(barrier, inc=1, device_id={"ma": peers[k]}, device_id_type=MESH)
    bl_peers = [lax.rem(my_bl + k, n_bl) for k in range(n_bl)]
    for k in range(1, n_bl):
        pl.semaphore_signal(barrier, inc=1, device_id={"bl": bl_peers[k]}, device_id_type=MESH)

    order_copy = pltpu.make_async_copy(order, order_s, small_sem.at[0])
    order_copy.start()
    starts = [c * per * LANES for c in range(CHUNKS)]
    sizes = [per * LANES] * (CHUNKS - 1) + [per * LANES + rem]
    vis_copies = []
    for c in range(CHUNKS):
        pieces = []
        for p in range(2):
            piece = pl.ds(starts[c], sizes[c])
            copy = pltpu.make_async_copy(vis.at[p, piece], vis_v.at[p, piece], vis_sem.at[c, p])
            copy.start()
            pieces.append(copy)
        vis_copies.append(pieces)
    pairs_copy = pltpu.make_async_copy(pairs, pairs_v, small_sem.at[1])
    pairs_copy.start()
    gains_copy = pltpu.make_async_copy(gains, gains_v, small_sem.at[2])
    gains_copy.start()
    beam_copies = []
    for c in range(CHUNKS):
        pieces = []
        for p in range(2):
            piece = pl.ds(starts[c], sizes[c])
            pieces.append(pltpu.make_async_copy(beam.at[0, p, piece], beam_v.at[p, piece], beam_sem.at[c, p]))
        beam_copies.append(pieces)

    order_copy.wait()
    slot = lax.broadcasted_iota(jnp.int32, (n_ma, LANES), 0)
    m_value = jnp.zeros((n_ma, LANES), jnp.int32)
    for j in range(n_ma):
        m_value = jnp.where(slot == j, order_s[j] - n_ma // 2, m_value)
    left, right = [], []
    for block in range(local_times // LANES):
        time = me * local_times + block * LANES + lax.broadcasted_iota(jnp.int32, (n_ma, LANES), 1)
        cos_k, sin_k = trig((time * m_value) & (NT - 1))
        scale = np.float32(1.0 / np.sqrt(np.float32(NT)))
        cos_k, sin_k = cos_k * scale, sin_k * scale
        left.append(jnp.concatenate([cos_k, -sin_k], axis=0).astype(jnp.bfloat16))
        right.append(jnp.concatenate([sin_k, cos_k], axis=0).astype(jnp.bfloat16))
    left = jnp.concatenate(left, axis=1)
    right = jnp.concatenate(right, axis=1)

    def transform(start, size):
        contract = (((1,), (1,)), ((), ()))
        re = lax.dot_general(left, vis_v[0, start:start + size, :], contract, preferred_element_type=jnp.float32)
        im = lax.dot_general(right, vis_v[1, start:start + size, :], contract, preferred_element_type=jnp.float32)
        return re + im

    sends = []
    for c in range(CHUNKS):
        for copy in vis_copies[c]:
            copy.wait()
        if c == CHUNKS - 1:
            for pieces in beam_copies:
                for copy in pieces:
                    copy.start()
        step = 2
        for i in range(0, per, step):
            flat = transform(starts[c] + i * LANES, step * LANES)
            for u in range(step):
                for p in range(2):
                    sums[c, pl.ds(p * per + i + u, n_ma, stride=2 * per), :] = (
                        flat[p * n_ma:(p + 1) * n_ma, u * LANES:(u + 1) * LANES]
                    )
        part[c] = sums[c].astype(jnp.bfloat16).reshape(n_ma, 2 * per, LANES)
        if c == 0:
            pl.semaphore_wait(barrier, n_ma - 1 + n_bl - 1)
        for k in order_of:
            copy = pltpu.make_async_remote_copy(
                src_ref=part.at[c, peers[k]], dst_ref=got.at[c, me],
                send_sem=send_sem.at[c, k], recv_sem=recv_sem.at[c, k],
                device_id={"ma": peers[k]}, device_id_type=MESH,
            )
            copy.start()
            sends.append((c, k, copy))
    flat = transform(cols * LANES, rem)
    wide = jnp.concatenate(
        [flat[:n_ma], flat[n_ma:], jnp.zeros((n_ma, LANES - 2 * rem), jnp.float32)], axis=1
    )
    for j in range(n_ma):
        rem_part[j] = wide[j:j + 1, :]
    for k in order_of:
        copy = pltpu.make_async_remote_copy(
            src_ref=rem_part.at[peers[k]], dst_ref=rem_got.at[me],
            send_sem=rem_send.at[k], recv_sem=rem_recv.at[k],
            device_id={"ma": peers[k]}, device_id_type=MESH,
        )
        copy.start()
        sends.append((CHUNKS, k, copy))

    pairs_copy.wait()
    gains_copy.wait()
    high = gains.shape[1] // LANES
    for comp in range(2):
        for h in range(high):
            table[comp * high + h:comp * high + h + 1, :] = gains_v[comp:comp + 1, h * LANES:(h + 1) * LANES]
    whole = table[...]
    first = whole.astype(jnp.bfloat16)
    rest = whole - first.astype(jnp.float32)
    second = rest.astype(jnp.bfloat16)
    third = (rest - second.astype(jnp.float32)).astype(jnp.bfloat16)
    thirds = jnp.concatenate([first, second, third], axis=0)

    def gain_of(feed, start, size):
        index = pairs_v[feed:feed + 1, start:start + size]
        low = lax.broadcasted_iota(jnp.int32, (LANES, size), 0)
        hot = jnp.where(low == (index & (LANES - 1)), 1.0, 0.0).astype(jnp.bfloat16)
        picked = jnp.dot(thirds, hot, preferred_element_type=jnp.float32)
        picked = picked[:2 * high] + picked[2 * high:4 * high] + picked[4 * high:]
        mask = lax.broadcasted_iota(jnp.int32, (high, size), 0) == index // LANES
        re = jnp.sum(jnp.where(mask, picked[:high], 0.0), axis=0, keepdims=True)
        im = jnp.sum(jnp.where(mask, picked[high:], 0.0), axis=0, keepdims=True)
        return re, im

    def factor_of(start, size):
        a_re, a_im = gain_of(0, start, size)
        b_re, b_im = gain_of(1, start, size)
        return a_re * b_re + a_im * b_im, a_im * b_re - a_re * b_im

    for i in range(0, cols, 2):
        f_re, f_im = factor_of(i * LANES, 2 * LANES)
        for u in range(2):
            factor[0, i + u:i + u + 1, :] = f_re[:, u * LANES:(u + 1) * LANES]
            factor[1, i + u:i + u + 1, :] = f_im[:, u * LANES:(u + 1) * LANES]
    rem_re, rem_im = factor_of(cols * LANES, rem)

    def weigh(s_re, s_im, f_re, f_im):
        s_re = s_re.astype(jnp.bfloat16).astype(jnp.float32)
        s_im = s_im.astype(jnp.bfloat16).astype(jnp.float32)
        return s_re * f_re - s_im * f_im, s_re * f_im + s_im * f_re

    total = None
    for c in range(CHUNKS):
        for copy in beam_copies[c]:
            copy.wait()
        mine = pl.multiple_of(me * 2 * per, 2 * per)
        spectra = sums[c, pl.ds(mine, 2 * per), :]
        for which, k, copy in sends:
            if which == c:
                copy.wait_recv()
        for k in range(1, n_ma):
            spectra = spectra + got[c, peers[k]].astype(jnp.float32)
        w_re, w_im = weigh(
            spectra[:per], spectra[per:], factor[0, c * per:(c + 1) * per], factor[1, c * per:(c + 1) * per]
        )
        for i in range(per):
            at = slice(starts[c] + i * LANES, starts[c] + (i + 1) * LANES)
            lhs[0:1, at] = w_re[i:i + 1]
            lhs[1:2, at] = w_im[i:i + 1]
        if c == CHUNKS - 1:
            for which, k, copy in sends:
                if which == CHUNKS:
                    copy.wait_recv()
            tail = rem_part[me]
            for k in range(1, n_ma):
                tail = tail + rem_got[peers[k]]
            w_re, w_im = weigh(tail[:, :rem], tail[:, rem:2 * rem], rem_re, rem_im)
            lhs[0:1, cols * LANES:rows] = w_re
            lhs[1:2, cols * LANES:rows] = w_im
        at = slice(starts[c], starts[c] + sizes[c])
        w_re, w_im = lhs[0:1, at], lhs[1:2, at]
        row_a = jnp.concatenate([w_re, w_im], axis=0).astype(jnp.bfloat16)
        row_b = jnp.concatenate([w_im, -w_re], axis=0).astype(jnp.bfloat16)
        term = jnp.dot(row_a, beam_v[0, at, :], preferred_element_type=jnp.float32)
        term = term + jnp.dot(row_b, beam_v[1, at, :], preferred_element_type=jnp.float32)
        total = term if total is None else total + term

    width = out.shape[2]
    for d in range(n_bl):
        share[d, :, 0:width] = total[:, d * width:(d + 1) * width]
    bl_copies = []
    for k in range(1, n_bl):
        copy = pltpu.make_async_remote_copy(
            src_ref=share.at[bl_peers[k]], dst_ref=share_got.at[my_bl],
            send_sem=bl_send.at[k], recv_sem=bl_recv.at[k],
            device_id={"bl": bl_peers[k]}, device_id_type=MESH,
        )
        copy.start()
        bl_copies.append(copy)
    for which, k, copy in sends:
        copy.wait_send()
    result = share[my_bl]
    for k in range(1, n_bl):
        bl_copies[k - 1].wait_recv()
    for k in range(1, n_bl):
        result = result + share_got[bl_peers[k]]
    out[:, 0, :] = result[:, :width]
    for copy in bl_copies:
        copy.wait_send()


def per_device(n_ma, n_bl, visibilities, beam_blocks, feed_pairs, feed_gains, m_order):
    _, rows, local_times = visibilities.shape
    width = beam_blocks.shape[3]
    assert m_order.shape[0] == n_ma and beam_blocks.shape[0] == 1
    cols = rows // LANES
    rem = rows - cols * LANES
    per = cols // CHUNKS
    assert cols % (2 * CHUNKS) == 0 and (2 * per) % 16 == 0 and 0 < 2 * rem <= LANES
    share_width = width // n_bl
    share_pad = -(-share_width // LANES) * LANES
    feeds = feed_gains.shape[1]
    f32, bf16 = jnp.float32, jnp.bfloat16
    dma = pltpu.SemaphoreType.DMA
    return pl.pallas_call(
        functools.partial(kernel, n_ma, n_bl),
        out_shape=jax.ShapeDtypeStruct((2, 1, share_width), f32),
        in_specs=[pl.BlockSpec(memory_space=pl.ANY)] * 5,
        out_specs=pl.BlockSpec(memory_space=pltpu.VMEM),
        scratch_shapes=[
            pltpu.VMEM((2, rows, local_times), bf16),
            pltpu.VMEM((2, rows, width), bf16),
            pltpu.VMEM((2, rows), jnp.int32),
            pltpu.VMEM((2, feeds), f32),
            pltpu.SMEM((n_ma,), jnp.int32),
            pltpu.VMEM((CHUNKS, n_ma * 2 * per, LANES), f32),
            pltpu.VMEM((CHUNKS, n_ma, 2 * per, LANES), bf16),
            pltpu.VMEM((CHUNKS, n_ma, 2 * per, LANES), bf16),
            pltpu.VMEM((n_ma, 1, LANES), f32),
            pltpu.VMEM((n_ma, 1, LANES), f32),
            pltpu.VMEM((2 * feeds // LANES, LANES), f32),
            pltpu.VMEM((2, cols, LANES), f32),
            pltpu.VMEM((8, rows), f32),
            pltpu.VMEM((n_bl, 2, share_pad), f32),
            pltpu.VMEM((n_bl, 2, share_pad), f32),
            dma((CHUNKS, 2)),
            dma((CHUNKS, 2)),
            dma((3,)),
            dma((CHUNKS, n_ma)),
            dma((CHUNKS, n_ma)),
            dma((n_ma,)),
            dma((n_ma,)),
            dma((n_bl,)),
            dma((n_bl,)),
        ],
        compiler_params=pltpu.CompilerParams(
            collective_id=0, has_side_effects=True, vmem_limit_bytes=56 * 2**20
        ),
        cost_estimate=pl.CostEstimate(
            flops=2 * rows * (2 * local_times * 2 * n_ma + 4 * width),
            bytes_accessed=4 * rows * (local_times + width),
            transcendentals=0,
        ),
    )(visibilities, beam_blocks, feed_pairs.T, feed_gains, m_order)


def solution(mesh):
    return jax.shard_map(
        functools.partial(per_device, mesh.shape["ma"], mesh.shape["bl"]),
        mesh=mesh,
        in_specs=(P(None, "bl", "ma"), P("ma", None, "bl", None), P("bl", None), P(), P()),
        out_specs=P(None, "ma", "bl"),
        check_vma=False,
    )
```

time: 91.2 us -> 18.6 us (0.20)
  blocking collectives: 71.1 us -> 0 us
  Pallas kernels: 0 us -> 17.1 us
  matrix products: 13.6 us -> 0 us
  local copies, waits for them, and re-layouts: 4.68 us -> 1.28 us
  other arithmetic: 1.49 us -> 0 us
    unnamed x1 -> x0, blocking collectives: 66.1 us -> none
    pallas_call x0 -> x1, Pallas kernels: none -> 17.1 us  [per_device(): pl.pallas_call(functools.partial(kernel, n_ma, n_bl), out_shape=jax.Shape...]
    dot_general x3 -> x0, matrix products: 13.6 us -> none  [the longest x1 7.6 us: per_device(): jnp.dot(one_hot, jnp.transpose(feed_gains), precision=lax.Precision.HIGHE...]
    psum x1 -> x0, blocking collectives: 4.97 us -> none  [per_device(): totals = lax.psum(partial_value, 'bl')]
    squeeze x1 -> x0, local copies, waits for them, and re-layouts: 2.52 us -> none  [transform(): stacked_in = jnp.concatenate([visible[0], visible[1]], axis=1)]
where the time goes in v1:
time: 18.6 us; the launch traced here: 18.4 us
  Pallas kernels  17.1 us (92%)
  local copies, waits for them, and re-layouts  1.28 us (7%)
    pallas_call x1, Pallas kernels, per_device(): pl.pallas_call(functools.partial(kernel, n_ma, n_bl), out_shape=jax.Shape...  17.1 us
    unnamed x1, local copies, waits for them, and re-layouts  1.28 us

profile of v1, /device:TPU:0, one launch (start us, length us, event | category | flops | bytes accessed | tf_op | source)
XLA Modules:
  0.0 18.4 jit_solution(18400370196268553029)
XLA Ops:
  0.0 17.1 %shard_map.55 = f32[2,1,500]{2,1,0:T(1,128)} custom-call(bf16[2,2080,512]{2,1,0:T(8,128)(2,1)} %vis.1, bf16[1,2,2080,1000]{3,2,1,0:T(8,128)(2,1)} %beam.1, s32[2,2080]{1,0:T(2,128)} %bitcast.1, f32[2,1024]{1,0:T(2,128)} %gains.1, s32[16]{0:T(128)} %order.1), custom_call_target="tpu_custom_call" | custom-call | flops 152954880 | bytes 12579840 | tf_op jit(solution)/shard_map/pallas_call | solution.py:262
  17.1 1.3 %copy.7 = f32[2,1,500]{2,1,0:T(1,128)} copy(f32[2,1,500]{2,1,0:T(1,128)} %shard_map.55) | data formatting | bytes 8000

commit v2 on v1

v2 whole, which is shorter than its diff:
```python
import functools

import jax
import jax.numpy as jnp
import numpy as np
from jax import lax
from jax.experimental import pallas as pl
from jax.experimental.pallas import tpu as pltpu
from jax.sharding import PartitionSpec as P

NT = 8192
LANES = 128
CHUNKS = 2
VMEM_LIMIT = 56 * 2**20
MESH = pl.DeviceIdType.MESH


def trig(k):
    quarter = NT // 4
    turn = (k + quarter // 2) // quarter
    x = (k - turn * quarter).astype(jnp.float32) * np.float32(2.0 * np.pi / NT)
    y = x * x
    sin_x = x * (1.0 + y * (-1.0 / 6 + y * (1.0 / 120 + y * (-1.0 / 5040 + y * (1.0 / 362880)))))
    cos_x = 1.0 + y * (-0.5 + y * (1.0 / 24 + y * (-1.0 / 720 + y * (1.0 / 40320))))
    odd = (turn & 1) == 1
    cos_k = jnp.where(odd, sin_x, cos_x)
    sin_k = jnp.where(odd, cos_x, sin_x)
    cos_k = jnp.where(((turn + 1) & 2) == 2, -cos_k, cos_k)
    sin_k = jnp.where((turn & 2) == 2, -sin_k, sin_k)
    return cos_k, sin_k


def kernel(
    n_ma, n_bl, vis, beam, pairs, gains, order, out,
    vis_v, beam_v, pairs_v, gains_v, order_s,
    sums, near, part, got, rem_sums, rem_near, rem_part, rem_got, table, factor, lhs, share,
    vis_sem, beam_sem, small_sem, near_send, near_recv, send_sem, recv_sem, bl_send, bl_recv,
):
    me = lax.axis_index("ma")
    my_bl = lax.axis_index("bl")
    rows = vis.shape[1]
    local_times = vis.shape[2]
    cols = rows // LANES
    rem = rows - cols * LANES
    per = cols // CHUNKS
    chips = n_ma // 2
    chip = me // 2
    core = lax.rem(me, 2)
    other = 1 - core
    sibling = chip * 2 + other
    far = [lax.rem(chip + k, chips) for k in range(chips)]
    far_order = sorted(range(1, chips), key=lambda k: abs(k - chips // 2))

    barrier = pltpu.get_barrier_semaphore()
    pl.semaphore_signal(barrier, inc=1, device_id={"ma": sibling}, device_id_type=MESH)
    for k in range(1, chips):
        pl.semaphore_signal(barrier, inc=1, device_id={"ma": far[k] * 2 + core}, device_id_type=MESH)
    bl_peers = [lax.rem(my_bl + k, n_bl) for k in range(n_bl)]
    for k in range(1, n_bl):
        pl.semaphore_signal(barrier, inc=1, device_id={"bl": bl_peers[k]}, device_id_type=MESH)

    order_copy = pltpu.make_async_copy(order, order_s, small_sem.at[0])
    order_copy.start()
    spans = [(c * per * LANES, per * LANES) for c in range(CHUNKS)] + [(cols * LANES, rem)]
    load_order = [0, CHUNKS] + list(range(1, CHUNKS))
    vis_copies, beam_copies = {}, {}
    for c in load_order:
        for p in range(2):
            piece = pl.ds(*spans[c])
            vis_copies[c, p] = pltpu.make_async_copy(vis.at[p, piece], vis_v.at[p, piece], vis_sem.at[c, p])
            vis_copies[c, p].start()
            beam_copies[c, p] = pltpu.make_async_copy(beam.at[0, p, piece], beam_v.at[p, piece], beam_sem.at[c, p])
    pairs_copy = pltpu.make_async_copy(pairs, pairs_v, small_sem.at[1])
    pairs_copy.start()
    gains_copy = pltpu.make_async_copy(gains, gains_v, small_sem.at[2])
    gains_copy.start()

    order_copy.wait()
    slot = lax.broadcasted_iota(jnp.int32, (n_ma, LANES), 0)
    m_value = jnp.zeros((n_ma, LANES), jnp.int32)
    for j in range(n_ma):
        m_value = jnp.where(slot == (j % 2) * chips + j // 2, order_s[j] - n_ma // 2, m_value)
    left, right = [], []
    for block in range(local_times // LANES):
        time = me * local_times + block * LANES + lax.broadcasted_iota(jnp.int32, (n_ma, LANES), 1)
        cos_k, sin_k = trig((time * m_value) & (NT - 1))
        scale = np.float32(1.0 / np.sqrt(np.float32(NT)))
        cos_k, sin_k = cos_k * scale, sin_k * scale
        left.append(jnp.concatenate([cos_k, -sin_k], axis=0).astype(jnp.bfloat16))
        right.append(jnp.concatenate([sin_k, cos_k], axis=0).astype(jnp.bfloat16))
    left = jnp.concatenate(left, axis=1)
    right = jnp.concatenate(right, axis=1)

    def transform(start, size):
        contract = (((1,), (1,)), ((), ()))
        re = lax.dot_general(left, vis_v[0, start:start + size, :], contract, preferred_element_type=jnp.float32)
        im = lax.dot_general(right, vis_v[1, start:start + size, :], contract, preferred_element_type=jnp.float32)
        return re + im

    near_copies = {}

    def to_sibling(c, source, target):
        near_copies[c] = pltpu.make_async_remote_copy(
            src_ref=source, dst_ref=target, send_sem=near_send.at[c], recv_sem=near_recv.at[c],
            device_id={"ma": sibling}, device_id_type=MESH,
        )
        near_copies[c].start()

    for c in load_order:
        for p in range(2):
            vis_copies[c, p].wait()
        if c == load_order[-1]:
            for b in load_order:
                for p in range(2):
                    beam_copies[b, p].start()
        if c == CHUNKS:
            flat = transform(*spans[c])
            wide = jnp.concatenate(
                [flat[:n_ma], flat[n_ma:], jnp.zeros((n_ma, LANES - 2 * rem), jnp.float32)], axis=1
            )
            for j in range(n_ma):
                rem_sums[j // chips, j % chips] = wide[j:j + 1, :]
            to_sibling(c, rem_sums.at[other], rem_near)
            continue
        step = 2
        for i in range(0, per, step):
            flat = transform(spans[c][0] + i * LANES, step * LANES)
            for u in range(step):
                for p in range(2):
                    for g in range(2):
                        from_row = p * n_ma + g * chips
                        sums[c, g, pl.ds(p * per + i + u, chips, stride=2 * per), :] = (
                            flat[from_row:from_row + chips, u * LANES:(u + 1) * LANES]
                        )
        if c == 0:
            pl.semaphore_wait(barrier, 1 + chips - 1 + n_bl - 1)
        to_sibling(c, sums.at[c, other], near.at[c])

    far_copies = {}
    for c in load_order:
        near_copies[c].wait_recv()
        if c == CHUNKS:
            rem_part[...] = rem_sums[core] + rem_near[...]
        else:
            both = sums[c, core] + near[c]
            sums[c, core] = both
            part[c] = both.astype(jnp.bfloat16).reshape(chips, 2 * per, LANES)
        for k in far_order:
            source = rem_part.at[far[k]] if c == CHUNKS else part.at[c, far[k]]
            target = rem_got.at[chip] if c == CHUNKS else got.at[c, chip]
            far_copies[c, k] = pltpu.make_async_remote_copy(
                src_ref=source, dst_ref=target, send_sem=send_sem.at[c, k], recv_sem=recv_sem.at[c, k],
                device_id={"ma": far[k] * 2 + core}, device_id_type=MESH,
            )
            far_copies[c, k].start()

    pairs_copy.wait()
    gains_copy.wait()
    high = gains.shape[1] // LANES
    for comp in range(2):
        for h in range(high):
            table[comp * high + h:comp * high + h + 1, :] = gains_v[comp:comp + 1, h * LANES:(h + 1) * LANES]
    whole = table[...]
    first = whole.astype(jnp.bfloat16)
    rest = whole - first.astype(jnp.float32)
    second = rest.astype(jnp.bfloat16)
    third = (rest - second.astype(jnp.float32)).astype(jnp.bfloat16)
    thirds = jnp.concatenate([first, second, third], axis=0)

    def gain_of(feed, start, size):
        index = pairs_v[feed:feed + 1, start:start + size]
        low = lax.broadcasted_iota(jnp.int32, (LANES, size), 0)
        hot = jnp.where(low == (index & (LANES - 1)), 1.0, 0.0).astype(jnp.bfloat16)
        picked = jnp.dot(thirds, hot, preferred_element_type=jnp.float32)
        picked = picked[:2 * high] + picked[2 * high:4 * high] + picked[4 * high:]
        mask = lax.broadcasted_iota(jnp.int32, (high, size), 0) == index // LANES
        re = jnp.sum(jnp.where(mask, picked[:high], 0.0), axis=0, keepdims=True)
        im = jnp.sum(jnp.where(mask, picked[high:], 0.0), axis=0, keepdims=True)
        return re, im

    def factor_of(start, size):
        a_re, a_im = gain_of(0, start, size)
        b_re, b_im = gain_of(1, start, size)
        return a_re * b_re + a_im * b_im, a_im * b_re - a_re * b_im

    for i in range(0, cols, 2):
        f_re, f_im = factor_of(i * LANES, 2 * LANES)
        for u in range(2):
            factor[0, i + u:i + u + 1, :] = f_re[:, u * LANES:(u + 1) * LANES]
            factor[1, i + u:i + u + 1, :] = f_im[:, u * LANES:(u + 1) * LANES]
    rem_re, rem_im = factor_of(*spans[CHUNKS])

    def weigh(s_re, s_im, f_re, f_im):
        s_re = s_re.astype(jnp.bfloat16).astype(jnp.float32)
        s_im = s_im.astype(jnp.bfloat16).astype(jnp.float32)
        return s_re * f_re - s_im * f_im, s_re * f_im + s_im * f_re

    total = None
    for c in load_order:
        for p in range(2):
            beam_copies[c, p].wait()
        for k in far_order:
            far_copies[c, k].wait_recv()
        start, size = spans[c]
        at = slice(start, start + size)
        if c == CHUNKS:
            tail = rem_part[chip]
            for k in far_order:
                tail = tail + rem_got[far[k]]
            w_re, w_im = weigh(tail[:, :rem], tail[:, rem:2 * rem], rem_re, rem_im)
            lhs[0:1, at] = w_re
            lhs[1:2, at] = w_im
        else:
            mine = pl.multiple_of(chip * 2 * per, 2 * per)
            spectra = sums[c, core, pl.ds(mine, 2 * per), :]
            for k in far_order:
                spectra = spectra + got[c, far[k]].astype(jnp.float32)
            w_re, w_im = weigh(
                spectra[:per], spectra[per:], factor[0, c * per:(c + 1) * per], factor[1, c * per:(c + 1) * per]
            )
            for i in range(per):
                lane = slice(start + i * LANES, start + (i + 1) * LANES)
                lhs[0:1, lane] = w_re[i:i + 1]
                lhs[1:2, lane] = w_im[i:i + 1]
        w_re, w_im = lhs[0:1, at], lhs[1:2, at]
        row_a = jnp.concatenate([w_re, w_im], axis=0).astype(jnp.bfloat16)
        row_b = jnp.concatenate([w_im, -w_re], axis=0).astype(jnp.bfloat16)
        term = jnp.dot(row_a, beam_v[0, at, :], preferred_element_type=jnp.float32)
        term = term + jnp.dot(row_b, beam_v[1, at, :], preferred_element_type=jnp.float32)
        total = term if total is None else total + term

    width = beam.shape[3] // n_bl
    for d in range(n_bl):
        share[d, :, 0, 0:width] = total[:, d * width:(d + 1) * width]
    bl_copies = []
    for k in range(1, n_bl):
        copy = pltpu.make_async_remote_copy(
            src_ref=share.at[bl_peers[k]], dst_ref=out.at[my_bl],
            send_sem=bl_send.at[k], recv_sem=bl_recv.at[k],
            device_id={"bl": bl_peers[k]}, device_id_type=MESH,
        )
        copy.start()
        bl_copies.append(copy)
    out[my_bl] = share[my_bl]
    for copy in near_copies.values():
        copy.wait_send()
    for copy in far_copies.values():
        copy.wait_send()
    for copy in bl_copies:
        copy.wait_send()
    for copy in bl_copies:
        copy.wait_recv()


def per_device(n_ma, n_bl, visibilities, beam_blocks, feed_pairs, feed_gains, m_order):
    _, rows, local_times = visibilities.shape
    width = beam_blocks.shape[3]
    assert m_order.shape[0] == n_ma and beam_blocks.shape[0] == 1 and n_ma % 16 == 0
    cols = rows // LANES
    rem = rows - cols * LANES
    per = cols // CHUNKS
    assert cols % (2 * CHUNKS) == 0 and (2 * per) % 16 == 0 and 0 < 2 * rem <= LANES
    chips = n_ma // 2
    share_width = width // n_bl
    share_pad = -(-share_width // LANES) * LANES
    feeds = feed_gains.shape[1]
    f32, bf16 = jnp.float32, jnp.bfloat16
    dma = pltpu.SemaphoreType.DMA
    parts = pl.pallas_call(
        functools.partial(kernel, n_ma, n_bl),
        out_shape=jax.ShapeDtypeStruct((n_bl, 2, 1, share_pad), f32),
        in_specs=[pl.BlockSpec(memory_space=pl.ANY)] * 5,
        out_specs=pl.BlockSpec(memory_space=pltpu.VMEM),
        scratch_shapes=[
            pltpu.VMEM((2, rows, local_times), bf16),
            pltpu.VMEM((2, rows, width), bf16),
            pltpu.VMEM((2, rows), jnp.int32),
            pltpu.VMEM((2, feeds), f32),
            pltpu.SMEM((n_ma,), jnp.int32),
            pltpu.VMEM((CHUNKS, 2, chips * 2 * per, LANES), f32),
            pltpu.VMEM((CHUNKS, chips * 2 * per, LANES), f32),
            pltpu.VMEM((CHUNKS, chips, 2 * per, LANES), bf16),
            pltpu.VMEM((CHUNKS, chips, 2 * per, LANES), bf16),
            pltpu.VMEM((2, chips, 1, LANES), f32),
            pltpu.VMEM((chips, 1, LANES), f32),
            pltpu.VMEM((chips, 1, LANES), f32),
            pltpu.VMEM((chips, 1, LANES), f32),
            pltpu.VMEM((2 * feeds // LANES, LANES), f32),
            pltpu.VMEM((2, cols, LANES), f32),
            pltpu.VMEM((8, rows), f32),
            pltpu.VMEM((n_bl, 2, 1, share_pad), f32),
            dma((CHUNKS + 1, 2)),
            dma((CHUNKS + 1, 2)),
            dma((3,)),
            dma((CHUNKS + 1,)),
            dma((CHUNKS + 1,)),
            dma((CHUNKS + 1, chips)),
            dma((CHUNKS + 1, chips)),
            dma((n_bl,)),
            dma((n_bl,)),
        ],
        compiler_params=pltpu.CompilerParams(
            collective_id=0, has_side_effects=True, vmem_limit_bytes=VMEM_LIMIT
        ),
        cost_estimate=pl.CostEstimate(
            flops=2 * rows * (2 * local_times * 2 * n_ma + 4 * width),
            bytes_accessed=4 * rows * (local_times + width),
            transcendentals=0,
        ),
    )(visibilities, beam_blocks, feed_pairs.T, feed_gains, m_order)
    return jnp.sum(parts[..., :share_width], axis=0)


def solution(mesh):
    return jax.shard_map(
        functools.partial(per_device, mesh.shape["ma"], mesh.shape["bl"]),
        mesh=mesh,
        in_specs=(P(None, "bl", "ma"), P("ma", None, "bl", None), P("bl", None), P(), P()),
        out_specs=P(None, "ma", "bl"),
        check_vma=False,
    )
```

time: 18.6 us -> 18.5 us (level)
  other arithmetic: 0 us -> 0.72 us
  local copies, waits for them, and re-layouts: 1.28 us -> 0.6 us
  Pallas kernels: 17.1 us -> 16.9 us
    unnamed x1 -> x0, local copies, waits for them, and re-layouts: 1.28 us -> none
    reduce_sum x0 -> x1, other arithmetic: none -> 0.72 us  [per_device(): return jnp.sum(parts[..., :share_width], axis=0)]
    reduce_sum x0 -> x1, local copies, waits for them, and re-layouts: none -> 0.6 us  [per_device(): return jnp.sum(parts[..., :share_width], axis=0)]
where the time goes in v2:
time: 18.5 us; the launch traced here: 18.3 us
  Pallas kernels  16.9 us (91%)
  other arithmetic  0.72 us (4%)
  local copies, waits for them, and re-layouts  0.6 us (3%)
    pallas_call x1, Pallas kernels, per_device(): pl.pallas_call(functools.partial(kernel, n_ma, n_bl), out_shape=jax.Shape...  16.9 us
    reduce_sum x1, other arithmetic, per_device(): return jnp.sum(parts[..., :share_width], axis=0)  0.72 us
    reduce_sum x1, local copies, waits for them, and re-layouts, per_device(): return jnp.sum(parts[..., :share_width], axis=0)  0.6 us

profile of v2, /device:TPU:0, one launch (start us, length us, event | category | flops | bytes accessed | tf_op | source)
XLA Modules:
  0.0 18.3 jit_solution(9126983545507484597)
XLA Ops:
  0.0 16.9 %shard_map.55 = f32[2,2,1,512]{3,2,1,0:T(1,128)} custom-call(bf16[2,2080,512]{2,1,0:T(8,128)(2,1)} %vis.1, bf16[1,2,2080,1000]{3,2,1,0:T(8,128)(2,1)} %beam.1, s32[2,2080]{1,0:T(2,128)} %bitcast.1, f32[2,1024]{1,0:T(2,128)} %gains.1, s32[16]{0:T(128)} %order.1), custom_call_target="tpu_custom_call" | custom-call | flops 152954880 | bytes 12579840 | tf_op jit(solution)/shard_map/pallas_call | solution.py:269
  16.9 0.7 %slice_reduce_fusion = f32[2,500]{1,0:T(2,128)S(1)} fusion(f32[2,2,1,512]{3,2,1,0:T(1,128)} %shard_map.55), kind=kLoop, calls=%fused_computation | loop fusion | flops 1000 | bytes 12000 | tf_op jit(solution)/shard_map/reduce_sum | solution.py:311
  17.7 0.6 %reduce_sum.12 = f32[2,1,500]{2,1,0:T(1,128)} reshape(f32[2,500]{1,0:T(2,128)S(1)} %slice_reduce_fusion) | data formatting | bytes 8000 | tf_op jit(solution)/shard_map/reduce_sum | solution.py:311

commit v3 on v2

--- a/solution.py
+++ b/solution.py
@@ -11,6 +11,7 @@
 NT = 8192
 LANES = 128
 CHUNKS = 2
+PIECE = 512
 VMEM_LIMIT = 56 * 2**20
 MESH = pl.DeviceIdType.MESH
 
@@ -63,23 +64,32 @@
     order_copy.start()
     spans = [(c * per * LANES, per * LANES) for c in range(CHUNKS)] + [(cols * LANES, rem)]
     load_order = [0, CHUNKS] + list(range(1, CHUNKS))
+    pieces = {}
+    for c in load_order:
+        start, size = spans[c]
+        pieces[c] = [(at, min(PIECE, start + size - at)) for at in range(start, start + size, PIECE)]
     vis_copies, beam_copies = {}, {}
+    slot = 0
     for c in load_order:
-        for p in range(2):
-            piece = pl.ds(*spans[c])
-            vis_copies[c, p] = pltpu.make_async_copy(vis.at[p, piece], vis_v.at[p, piece], vis_sem.at[c, p])
-            vis_copies[c, p].start()
-            beam_copies[c, p] = pltpu.make_async_copy(beam.at[0, p, piece], beam_v.at[p, piece], beam_sem.at[c, p])
+        for at, size in pieces[c]:
+            for p in range(2):
+                piece = pl.ds(at, size)
+                vis_copies[at, p] = pltpu.make_async_copy(vis.at[p, piece], vis_v.at[p, piece], vis_sem.at[slot])
+                vis_copies[at, p].start()
+                beam_copies[at, p] = pltpu.make_async_copy(
+                    beam.at[0, p, piece], beam_v.at[p, piece], beam_sem.at[slot]
+                )
+                slot += 1
     pairs_copy = pltpu.make_async_copy(pairs, pairs_v, small_sem.at[1])
     pairs_copy.start()
     gains_copy = pltpu.make_async_copy(gains, gains_v, small_sem.at[2])
     gains_copy.start()
 
     order_copy.wait()
-    slot = lax.broadcasted_iota(jnp.int32, (n_ma, LANES), 0)
+    row_of = lax.broadcasted_iota(jnp.int32, (n_ma, LANES), 0)
     m_value = jnp.zeros((n_ma, LANES), jnp.int32)
     for j in range(n_ma):
-        m_value = jnp.where(slot == (j % 2) * chips + j // 2, order_s[j] - n_ma // 2, m_value)
+        m_value = jnp.where(row_of == (j % 2) * chips + j // 2, order_s[j] - n_ma // 2, m_value)
     left, right = [], []
     for block in range(local_times // LANES):
         time = me * local_times + block * LANES + lax.broadcasted_iota(jnp.int32, (n_ma, LANES), 1)
@@ -106,38 +116,9 @@
         )
         near_copies[c].start()
 
-    for c in load_order:
-        for p in range(2):
-            vis_copies[c, p].wait()
-        if c == load_order[-1]:
-            for b in load_order:
-                for p in range(2):
-                    beam_copies[b, p].start()
-        if c == CHUNKS:
-            flat = transform(*spans[c])
-            wide = jnp.concatenate(
-                [flat[:n_ma], flat[n_ma:], jnp.zeros((n_ma, LANES - 2 * rem), jnp.float32)], axis=1
-            )
-            for j in range(n_ma):
-                rem_sums[j // chips, j % chips] = wide[j:j + 1, :]
-            to_sibling(c, rem_sums.at[other], rem_near)
-            continue
-        step = 2
-        for i in range(0, per, step):
-            flat = transform(spans[c][0] + i * LANES, step * LANES)
-            for u in range(step):
-                for p in range(2):
-                    for g in range(2):
-                        from_row = p * n_ma + g * chips
-                        sums[c, g, pl.ds(p * per + i + u, chips, stride=2 * per), :] = (
-                            flat[from_row:from_row + chips, u * LANES:(u + 1) * LANES]
-                        )
-        if c == 0:
-            pl.semaphore_wait(barrier, 1 + chips - 1 + n_bl - 1)
-        to_sibling(c, sums.at[c, other], near.at[c])
-
     far_copies = {}
-    for c in load_order:
+
+    def to_far(c):
         near_copies[c].wait_recv()
         if c == CHUNKS:
             rem_part[...] = rem_sums[core] + rem_near[...]
@@ -154,6 +135,44 @@
             )
             far_copies[c, k].start()
 
+    waiting = []
+    for c in load_order:
+        for number, (at, size) in enumerate(pieces[c]):
+            for p in range(2):
+                vis_copies[at, p].wait()
+            if c == 0 and number == len(pieces[c]) - 1:
+                for copy in beam_copies.values():
+                    copy.start()
+            if c == CHUNKS:
+                flat = transform(at, size)
+                wide = jnp.concatenate(
+                    [flat[:n_ma], flat[n_ma:], jnp.zeros((n_ma, LANES - 2 * rem), jnp.float32)], axis=1
+                )
+                for j in range(n_ma):
+                    rem_sums[j // chips, j % chips] = wide[j:j + 1, :]
+                continue
+            for begin in range(at, at + size, 2 * LANES):
+                flat = transform(begin, 2 * LANES)
+                for u in range(2):
+                    row = (begin - spans[c][0]) // LANES + u
+                    for p in range(2):
+                        for g in range(2):
+                            from_row = p * n_ma + g * chips
+                            sums[c, g, pl.ds(p * per + row, chips, stride=2 * per), :] = (
+                                flat[from_row:from_row + chips, u * LANES:(u + 1) * LANES]
+                            )
+            if number == 0:
+                for b in waiting:
+                    to_far(b)
+                waiting = []
+        if c == 0:
+            pl.semaphore_wait(barrier, 1 + chips - 1 + n_bl - 1)
+        if c == CHUNKS:
+            to_sibling(c, rem_sums.at[other], rem_near)
+        else:
+            to_sibling(c, sums.at[c, other], near.at[c])
+        waiting.append(c)
+
     pairs_copy.wait()
     gains_copy.wait()
     high = gains.shape[1] // LANES
@@ -190,6 +209,9 @@
             factor[1, i + u:i + u + 1, :] = f_im[:, u * LANES:(u + 1) * LANES]
     rem_re, rem_im = factor_of(*spans[CHUNKS])
 
+    for b in waiting:
+        to_far(b)
+
     def weigh(s_re, s_im, f_re, f_im):
         s_re = s_re.astype(jnp.bfloat16).astype(jnp.float32)
         s_im = s_im.astype(jnp.bfloat16).astype(jnp.float32)
@@ -197,8 +219,6 @@
 
     total = None
     for c in load_order:
-        for p in range(2):
-            beam_copies[c, p].wait()
         for k in far_order:
             far_copies[c, k].wait_recv()
         start, size = spans[c]
@@ -222,12 +242,17 @@
                 lane = slice(start + i * LANES, start + (i + 1) * LANES)
                 lhs[0:1, lane] = w_re[i:i + 1]
                 lhs[1:2, lane] = w_im[i:i + 1]
-        w_re, w_im = lhs[0:1, at], lhs[1:2, at]
-        row_a = jnp.concatenate([w_re, w_im], axis=0).astype(jnp.bfloat16)
-        row_b = jnp.concatenate([w_im, -w_re], axis=0).astype(jnp.bfloat16)
-        term = jnp.dot(row_a, beam_v[0, at, :], preferred_element_type=jnp.float32)
-        term = term + jnp.dot(row_b, beam_v[1, at, :], preferred_element_type=jnp.float32)
-        total = term if total is None else total + term
+        for begin, size in pieces[c]:
+            at = slice(begin, begin + size)
+            w_re, w_im = lhs[0:1, at], lhs[1:2, at]
+            rows_of = [
+                jnp.concatenate([w_re, w_im], axis=0).astype(jnp.bfloat16),
+                jnp.concatenate([w_im, -w_re], axis=0).astype(jnp.bfloat16),
+            ]
+            for p in range(2):
+                beam_copies[begin, p].wait()
+                term = jnp.dot(rows_of[p], beam_v[p, at, :], preferred_element_type=jnp.float32)
+                total = term if total is None else total + term
 
     width = beam.shape[3] // n_bl
     for d in range(n_bl):
@@ -259,7 +284,7 @@
     cols = rows // LANES
     rem = rows - cols * LANES
     per = cols // CHUNKS
-    assert cols % (2 * CHUNKS) == 0 and (2 * per) % 16 == 0 and 0 < 2 * rem <= LANES
+    assert per * LANES % PIECE == 0 and cols % CHUNKS == 0 and (2 * per) % 16 == 0 and 0 < 2 * rem <= LANES
     chips = n_ma // 2
     share_width = width // n_bl
     share_pad = -(-share_width // LANES) * LANES
@@ -289,8 +314,8 @@
             pltpu.VMEM((2, cols, LANES), f32),
             pltpu.VMEM((8, rows), f32),
             pltpu.VMEM((n_bl, 2, 1, share_pad), f32),
-            dma((CHUNKS + 1, 2)),
-            dma((CHUNKS + 1, 2)),
+            dma((2 * (cols * LANES // PIECE + 1),)),
+            dma((2 * (cols * LANES // PIECE + 1),)),
             dma((3,)),
             dma((CHUNKS + 1,)),
             dma((CHUNKS + 1,)),
@@ -308,7 +333,10 @@
             transcendentals=0,
         ),
     )(visibilities, beam_blocks, feed_pairs.T, feed_gains, m_order)
-    return jnp.sum(parts[..., :share_width], axis=0)
+    result = parts[0, :, :, :share_width]
+    for d in range(1, n_bl):
+        result = result + parts[d, :, :, :share_width]
+    return result
 
 
 def solution(mesh):

time: 18.5 us -> 19.1 us (1.032)
  Pallas kernels: 16.9 us -> 17.6 us
  local copies, waits for them, and re-layouts: 0.6 us -> 0 us
  other arithmetic: 0.72 us -> 1.28 us
    add x0 -> x1, other arithmetic: none -> 1.28 us  [per_device(): result = result + parts[d, :, :, :share_width]]
    reduce_sum x1 -> x0, other arithmetic: 0.72 us -> none  [per_device(): return jnp.sum(parts[..., :share_width], axis=0)]
    pallas_call x1, Pallas kernels: 16.9 us -> 17.6 us  [per_device(): pl.pallas_call(functools.partial(kernel, n_ma, n_bl), out_shape=jax.Shape...]
    reduce_sum x1 -> x0, local copies, waits for them, and re-layouts: 0.6 us -> none  [per_device(): return jnp.sum(parts[..., :share_width], axis=0)]
where the time goes in v3:
time: 19.1 us; the launch traced here: 18.9 us
  Pallas kernels  17.6 us (92%)
  other arithmetic  1.28 us (7%)
    pallas_call x1, Pallas kernels, per_device(): pl.pallas_call(functools.partial(kernel, n_ma, n_bl), out_shape=jax.Shape...  17.6 us
    add x1, other arithmetic, per_device(): result = result + parts[d, :, :, :share_width]  1.28 us

profile of v3, /device:TPU:0, one launch (start us, length us, event | category | flops | bytes accessed | tf_op | source)
XLA Modules:
  0.0 18.9 jit_solution(3577503513332213468)
XLA Ops:
  0.0 17.6 %shard_map.55 = f32[2,2,1,512]{3,2,1,0:T(1,128)} custom-call(bf16[2,2080,512]{2,1,0:T(8,128)(2,1)} %vis.1, bf16[1,2,2080,1000]{3,2,1,0:T(8,128)(2,1)} %beam.1, s32[2,2080]{1,0:T(2,128)} %bitcast.3, f32[2,1024]{1,0:T(2,128)} %gains.1, s32[16]{0:T(128)} %order.1), custom_call_target="tpu_custom_call" | custom-call | flops 152954880 | bytes 12579840 | tf_op jit(solution)/shard_map/pallas_call | solution.py:294
  17.6 1.3 %add_bitcast_fusion = f32[2,1,500]{2,1,0:T(1,128)} fusion(f32[2,2,1,512]{3,2,1,0:T(1,128)} %shard_map.55), kind=kLoop, calls=%fused_computation | loop fusion | flops 1000 | bytes 12000 | tf_op jit(solution)/shard_map/add | solution.py:338
